TPU v7x, 128 devices: a whole 4x4x4 slice. The times are simulated.
128 devices in a mesh: tx: 8 (over x, core), ty: 16 (over z, y).
Axes of the slice: x: 4, y: 4, z: 4, core: 2. Of those that a mesh axis runs over, the one named last changes fastest.
Arguments:
- solution: float32 [4, 1024, 4096], P(None, 'tx', 'ty'), may hold values from -6 to 6
- residual: float32 [4, 1024, 4096], P(None, 'tx', 'ty')
- direction: float32 [4, 1024, 4096], P(None, 'tx', 'ty')
- blocks: bfloat16 [32768, 128, 256], P(('tx', 'ty')), may hold values from -0.375 to 0.375
- bin_owner: int32 [32768, 1], P(('tx', 'ty')), may hold values from 0 to 127; in each aligned block of 256 rows (0 to 255, 256 to 511, ...) at most 3 rows name the same one
- bin_tile: int32 [32768], P(('tx', 'ty')), may hold values from 0 to 127
Outputs:
- next_solution: float32 [4, 1024, 4096], P(None, 'tx', 'ty')
- next_residual: float32 [4, 1024, 4096], P(None, 'tx', 'ty')
- next_direction: float32 [4, 1024, 4096], P(None, 'tx', 'ty')
Inputs may be any that keep to these rules, and one draw needn't show every extreme that they name: `bin_owner`: among the bins of one device, at most 3 name the same owner, and on some devices some owner is named by exactly 3 of them.
All inputs are finite; a program needn't handle non-finite values.
Results may differ from a plain program's by a relative error of at most 0.0024.
Values may be sent and summed in bfloat16 or wider, within the bound.
A program may use at most 128 MiB of HBM per device.

v0:
```python
import jax
import jax.numpy as jnp
from jax import lax
from jax.sharding import PartitionSpec as P

TILE_SIDE = 16
smooth_weight = 0.25


def padded_2(shard, sides, width):
    for axis, dim in sides:
        size, length = (lax.axis_size(axis), shard.shape[dim])
        up = [(i, (i + 1) % size) for i in range(size - 1)]
        down = [(j, i) for i, j in up]
        last = lax.slice_in_dim(shard, length - width, length, axis=dim)
        initial = lax.slice_in_dim(shard, 0, width, axis=dim)
        before = lax.ppermute(last, axis, up)
        after = lax.ppermute(initial, axis, down)
        shard = jnp.concatenate([before, shard, after], axis=dim)
    return shard


def to_tiles(field):
    beacons, rows, cols = field.shape
    across = rows // TILE_SIDE
    down = cols // TILE_SIDE
    shaped = field.reshape(beacons, across, TILE_SIDE, down, TILE_SIDE).transpose(1, 3, 0, 2, 4)
    return shaped.reshape(across * down, beacons, TILE_SIDE * TILE_SIDE)


def to_field(tiles, rows, cols):
    beacons = tiles.shape[1]
    across = rows // TILE_SIDE
    down = cols // TILE_SIDE
    shaped = tiles.reshape(across, down, beacons, TILE_SIDE, TILE_SIDE).transpose(2, 0, 3, 1, 4)
    return shaped.reshape(beacons, rows, cols)


def laplace_local(field):
    padded = padded_2(field.astype(jnp.bfloat16), (("tx", 1), ("ty", 2)), 1).astype(field.dtype)
    near = padded[:, 2:, 1:-1] + padded[:, :-2, 1:-1] + padded[:, 1:-1, 2:] + padded[:, 1:-1, :-2]
    return 4.0 * field - near


def per_device(solution, residual, direction, blocks, bin_owner, bin_tile):
    beacons, rows, cols = direction.shape
    cells = TILE_SIDE * TILE_SIDE
    across_x = lax.axis_size("tx")
    across_y = lax.axis_size("ty")
    devices = across_x * across_y
    count = blocks.shape[0]
    cap = max(2, 3 * count // (2 * devices))
    owner = bin_owner[:, 0]
    member = (owner[:, None] == jnp.arange(devices, dtype=jnp.int32)[None, :]).astype(jnp.int32)
    before = jnp.cumsum(member, axis=0) - member
    rank = jnp.sum(before * member, axis=1)
    slot = owner * cap + rank
    request = jnp.full((devices * cap,), -1, jnp.int32).at[slot].set(bin_tile)
    wanted = lax.all_to_all(
        request.reshape(devices, cap), ("tx", "ty"), split_axis=0, concat_axis=0, tiled=True
    )
    wanted = jnp.maximum(wanted.reshape(devices * cap), 0)
    own_tiles = to_tiles(direction.astype(jnp.bfloat16))
    outgoing = jnp.take(own_tiles, wanted, axis=0)
    fetched = lax.all_to_all(
        outgoing.reshape(devices, cap, beacons, cells),
        ("tx", "ty"),
        split_axis=0,
        concat_axis=0,
        tiled=True,
    )
    fetched = fetched.reshape(devices * cap, beacons, cells)
    picked = jnp.take(fetched, slot, axis=0)
    samples = jnp.einsum("bsc,bkc->bks", blocks, picked, preferred_element_type=jnp.float32).astype(
        jnp.bfloat16
    )
    adjoint = jnp.einsum("bsc,bks->bkc", blocks, samples, preferred_element_type=jnp.float32)
    returned = jnp.zeros((devices * cap, beacons, cells), jnp.float32).at[slot].set(adjoint)
    arrived = lax.all_to_all(
        returned.reshape(devices, cap, beacons, cells),
        ("tx", "ty"),
        split_axis=0,
        concat_axis=0,
        tiled=True,
    )
    arrived = arrived.reshape(devices * cap, beacons, cells)
    data_tiles = jnp.zeros(own_tiles.shape, jnp.float32).at[wanted].add(arrived)
    image = to_field(data_tiles, rows, cols) + smooth_weight * laplace_local(direction)
    norm_old = lax.psum(jnp.sum(residual * residual, axis=(1, 2)), ("tx", "ty"))
    curvature = lax.psum(jnp.sum(direction * image, axis=(1, 2)), ("tx", "ty"))
    alpha = norm_old / curvature
    next_residual = residual - alpha[:, None, None] * image
    norm_new = lax.psum(jnp.sum(next_residual * next_residual, axis=(1, 2)), ("tx", "ty"))
    next_solution = solution + alpha[:, None, None] * direction
    next_direction = next_residual + (norm_new / norm_old)[:, None, None] * direction
    return (next_solution, next_residual, next_direction)


def solution(mesh):
    placed = (
        P(None, "tx", "ty"),
        P(None, "tx", "ty"),
        P(None, "tx", "ty"),
        P(("tx", "ty"), None, None),
        P(("tx", "ty"), None),
        P(("tx", "ty")),
    )
    return jax.shard_map(
        per_device,
        mesh=mesh,
        in_specs=placed,
        out_specs=(P(None, "tx", "ty"), P(None, "tx", "ty"), P(None, "tx", "ty")),
        check_vma=False,
    )
```

profile of v0, /device:TPU:1, one launch (start us, length us, event | category | flops | bytes accessed | tf_op | source)
XLA Modules:
  0.0 294.0 jit_solution(3272720926653905522)
XLA Ops:
  3.3 1.6 scatter_custom_fusion
  5.7 11.5 %all-to-all-start = ((s32[128,1,3]{2,1,0:T(1,128)}), s32[128,1,3]{2,1,0:T(1,128)S(1)}, u32[]{:S(2)}, u32[]{:S(2)}) async-start(s32[128,1,3]{2,1,0:T(1,128)} %bitcast.7), calls=%async_computation | async-start | bytes 131072 | tf_op jit(solution)/shard_map/all_to_all | solution.py:59
  18.3 2.5 reshape.85
  20.7 2.1 copy.33
  22.9 2.0 reshape.86
  25.1 1.8 all-to-all-done
  27.7 2.3 gather_fusion
  30.0 1.4 broadcast_select_fusion
  31.4 8.0 %all-to-all-start.1 = ((bf16[128,3,4,256]{3,2,1,0:T(4,128)(2,1)}), bf16[128,3,4,256]{3,2,1,0:T(4,128)(2,1)S(1)}, u32[]{:S(2)}, u32[]{:S(2)}) async-start(bf16[128,3,4,256]{3,2,1,0:T(4,128)(2,1)} %broadcast_select_fusion), calls=%async_computation.1 | async-start | bytes 1572864 | tf_op jit(solution)/shard_map/all_to_all | solution.py:65
  39.5 16.6 %all-to-all-done.1 = bf16[128,3,4,256]{3,2,1,0:T(4,128)(2,1)S(1)} async-done(((bf16[128,3,4,256]{3,2,1,0:T(4,128)(2,1)}), bf16[128,3,4,256]{3,2,1,0:T(4,128)(2,1)S(1)}, u32[]{:S(2)}, u32[]{:S(2)}) %all-to-all-start.1) | async-done | bytes 786464 | tf_op jit(solution)/shard_map/all_to_all | solution.py:65
  57.3 16.9 %fusion = f32[256,4,256]{2,1,0:T(4,128)S(1)} fusion(bf16[256,128,256]{2,1,0:T(8,128)(2,1)} %param.9, bf16[256,4,256]{2,1,0:T(4,128)(2,1)S(1)} %gather_fusion.1, pred[256]{0:T(512)(128)(4,1)S(1)} %get-tuple-element.9), kind=kOutput, calls=%fused_computation.8 | convolution fusion | flops 134610944 | bytes 18350336 | tf_op jit(solution)/shard_map/bsc,bks->bkc/dot_general | solution.py:77
  75.5 23.9 %scatter_fusion = f32[384,4,256]{2,1,0:T(4,128)} fusion(f32[384,4,256]{2,1,0:T(4,128)} %broadcast_in_dim.38, s32[256]{0:T(256)S(1)} %bitcast.49, f32[256,4,256]{2,1,0:T(4,128)S(1)} %fusion), kind=kCustom, calls=%fused_computation.3 | custom fusion | bytes 3146752 | tf_op jit(solution)/shard_map/scatter | solution.py:78
  99.4 4.2 %all-to-all-start.2 = ((f32[128,3,4,256]{3,2,1,0:T(4,128)}), f32[128,3,4,256]{3,2,1,0:T(4,128)S(1)}, u32[]{:S(2)}, u32[]{:S(2)}) async-start(f32[128,3,4,256]{3,2,1,0:T(4,128)} %bitcast.12), calls=%async_computation.2 | async-start | bytes 3145728 | tf_op jit(solution)/shard_map/all_to_all | solution.py:79
  103.6 3.1 %collective-permute-start.1 = (bf16[4,1,256]{2,1,0:T(2,128)(2,1)S(1)}, bf16[4,1,256]{2,1,0:T(2,128)(2,1)S(1)}, u32[]{:S(2)}, u32[]{:S(2)}) collective-permute-start(bf16[4,1,256]{2,1,0:T(2,128)(2,1)S(1)} %get-tuple-element.16), channel_id=1, source_target_pairs={{16,0},{32,16},{48,32},{64,48},{80,64},{96,80},{112,96},{17,1},{33... | collective-permute-start | bytes 6152 | tf_op jit(solution)/shard_map/ppermute | solution.py:18
  106.7 2.4 collective-permute-start
  109.2 13.3 %collective-permute-done.1 = bf16[4,1,256]{2,1,0:T(2,128)(2,1)S(1)} collective-permute-done((bf16[4,1,256]{2,1,0:T(2,128)(2,1)S(1)}, bf16[4,1,256]{2,1,0:T(2,128)(2,1)S(1)}, u32[]{:S(2)}, u32[]{:S(2)}) %collective-permute-start.1) | collective-permute-done | bytes 2080 | tf_op jit(solution)/shard_map/ppermute | solution.py:18
  122.7 1.5 collective-permute-start.3
  124.1 4.0 %collective-permute-start.2 = (bf16[4,130,1]{2,1,0:T(8,128)(2,1)S(1)}, bf16[4,130,1]{2,1,0:T(8,128)(2,1)S(1)}, u32[]{:S(2)}, u32[]{:S(2)}) collective-permute-start(bf16[4,130,1]{2,1,0:T(8,128)(2,1)S(1)} %get-tuple-element.13), channel_id=1, source_target_pairs={{0,1},{1,2},{2,3},{3,4},{4,5},{5,6},{6,7},{7,8},{8,9},{9,10},{10,1... | collective-permute-start | bytes 3128 | tf_op jit(solution)/shard_map/ppermute | solution.py:17
  130.5 14.7 %scatter_fusion.1 = f32[128,4,256]{2,1,0:T(4,128)S(1)} fusion(f32[128,4,256]{2,1,0:T(4,128)S(1)} %broadcast_in_dim.36, s32[384]{0:T(512)S(1)} %reshape.126, f32[384,4,256]{2,1,0:T(4,128)S(1)} %bitcast.39), kind=kCustom, calls=%fused_computation.4 | custom fusion | flops 393216 | bytes 4720128 | tf_op jit(solution)/shard_map/scatter-add | solution.py:87
  145.3 2.6 reshape.90
  148.0 5.9 %copy.31 = f32[4,8,16,16,16]{4,3,2,1,0:T(8,128)} copy(f32[4,8,16,16,16]{4,2,3,1,0:T(8,128)} %bitcast.37) | data formatting | bytes 1048576 | tf_op jit(solution)/shard_map/transpose | solution.py:35
  153.8 3.6 %reshape.91 = f32[4,128,256]{2,1,0:T(8,128)S(1)} reshape(f32[4,8,16,16,16]{4,3,2,1,0:T(8,128)} %copy.31) | data formatting | bytes 1048576 | tf_op jit(solution)/shard_map/reshape | solution.py:36
  158.0 72.0 %all-reduce = (f32[4]{0:T(128)S(1)}, f32[4]{0:T(128)S(1)}) all-reduce(f32[4]{0:T(128)S(1)} %get-tuple-element.17, f32[4]{0:T(128)S(1)} %get-tuple-element.7), channel_id=1, replica_groups=mesh['tx'=8,'ty'=16] {'tx','ty'}, use_global_device_ids=true, to_apply=%region_1.2 | all-reduce | flops 8 | bytes 64 | tf_op jit(solution)/shard_map/psum | solution.py:89
  230.3 62.5 %psum.23 = f32[4]{0:T(128)S(1)} all-reduce(f32[4]{0:T(128)S(1)} %get-tuple-element.5), channel_id=1, replica_groups=mesh['tx'=8,'ty'=16] {'tx','ty'}, use_global_device_ids=true, to_apply=%region_11.12 | all-reduce | flops 4 | bytes 32 | tf_op jit(solution)/shard_map/psum | solution.py:93
  (45 shorter events, 12.7 us)
Async XLA Ops:
  5.7 21.2 %all-to-all-start = ((s32[128,1,3]{2,1,0:T(1,128)}), s32[128,1,3]{2,1,0:T(1,128)S(1)}, u32[]{:S(2)}, u32[]{:S(2)}) async-start(s32[128,1,3]{2,1,0:T(1,128)} %bitcast.7), calls=%async_computation | async-start | bytes 131072 | tf_op jit(solution)/shard_map/all_to_all | solution.py:59
  31.4 24.7 %all-to-all-start.1 = ((bf16[128,3,4,256]{3,2,1,0:T(4,128)(2,1)}), bf16[128,3,4,256]{3,2,1,0:T(4,128)(2,1)S(1)}, u32[]{:S(2)}, u32[]{:S(2)}) async-start(bf16[128,3,4,256]{3,2,1,0:T(4,128)(2,1)} %broadcast_select_fusion), calls=%async_computation.1 | async-start | bytes 1572864 | tf_op jit(solution)/shard_map/all_to_all | solution.py:65
  99.4 31.1 %all-to-all-start.2 = ((f32[128,3,4,256]{3,2,1,0:T(4,128)}), f32[128,3,4,256]{3,2,1,0:T(4,128)S(1)}, u32[]{:S(2)}, u32[]{:S(2)}) async-start(f32[128,3,4,256]{3,2,1,0:T(4,128)} %bitcast.12), calls=%async_computation.2 | async-start | bytes 3145728 | tf_op jit(solution)/shard_map/all_to_all | solution.py:79
  103.6 18.9 %collective-permute-start.1 = (bf16[4,1,256]{2,1,0:T(2,128)(2,1)S(1)}, bf16[4,1,256]{2,1,0:T(2,128)(2,1)S(1)}, u32[]{:S(2)}, u32[]{:S(2)}) collective-permute-start(bf16[4,1,256]{2,1,0:T(2,128)(2,1)S(1)} %get-tuple-element.16), channel_id=1, source_target_pairs={{16,0},{32,16},{48,32},{64,48},{80,64},{96,80},{112,96},{17,1},{33... | collective-permute-start | bytes 6152 | tf_op jit(solution)/shard_map/ppermute | solution.py:18
  106.7 15.7 %collective-permute-start = (bf16[4,1,256]{2,1,0:T(2,128)(2,1)S(1)}, bf16[4,1,256]{2,1,0:T(2,128)(2,1)S(1)}, u32[]{:S(2)}, u32[]{:S(2)}) collective-permute-start(bf16[4,1,256]{2,1,0:T(2,128)(2,1)S(1)} %get-tuple-element.15), channel_id=1, source_target_pairs={{0,16},{16,32},{32,48},{48,64},{64,80},{80,96},{96,112},{1,17},{17... | collective-permute-start | bytes 6152 | tf_op jit(solution)/shard_map/ppermute | solution.py:17
  122.7 6.1 %collective-permute-start.3 = (bf16[4,130,1]{2,1,0:T(8,128)(2,1)S(1)}, bf16[4,130,1]{2,1,0:T(8,128)(2,1)S(1)}, u32[]{:S(2)}, u32[]{:S(2)}) collective-permute-start(bf16[4,130,1]{2,1,0:T(8,128)(2,1)S(1)} %get-tuple-element.14), channel_id=1, source_target_pairs={{1,0},{2,1},{3,2},{4,3},{5,4},{6,5},{7,6},{8,7},{9,8},{10,9},{11,1... | collective-permute-start | bytes 3128 | tf_op jit(solution)/shard_map/ppermute | solution.py:18
  124.1 6.0 %collective-permute-start.2 = (bf16[4,130,1]{2,1,0:T(8,128)(2,1)S(1)}, bf16[4,130,1]{2,1,0:T(8,128)(2,1)S(1)}, u32[]{:S(2)}, u32[]{:S(2)}) collective-permute-start(bf16[4,130,1]{2,1,0:T(8,128)(2,1)S(1)} %get-tuple-element.13), channel_id=1, source_target_pairs={{0,1},{1,2},{2,3},{3,4},{4,5},{5,6},{6,7},{7,8},{8,9},{9,10},{10,1... | collective-permute-start | bytes 3128 | tf_op jit(solution)/shard_map/ppermute | solution.py:17
  153.8 3.6 %copy-start = (f32[4,128,256]{2,1,0:T(8,128)S(1)}, f32[4,128,256]{2,1,0:T(8,128)}, u32[]{:S(2)}) copy-start(f32[4,128,256]{2,1,0:T(8,128)} %param.8) | copy-start | bytes 1572868
  153.8 3.6 %copy-start.1 = (f32[4,128,256]{2,1,0:T(8,128)S(1)}, f32[4,128,256]{2,1,0:T(8,128)}, u32[]{:S(2)}) copy-start(f32[4,128,256]{2,1,0:T(8,128)} %param.7) | copy-start | bytes 1572868
  157.5 135.4 %copy-start.3 = (f32[4,128,256]{2,1,0:T(8,128)S(1)}, f32[4,128,256]{2,1,0:T(8,128)}, u32[]{:S(2)}) copy-start(f32[4,128,256]{2,1,0:T(8,128)} %param.6) | copy-start | bytes 1572868
  230.3 63.7 %copy-start.2 = (f32[4,128,256]{2,1,0:T(8,128)}, f32[4,128,256]{2,1,0:T(8,128)S(1)}, u32[]{:S(2)}) copy-start(f32[4,128,256]{2,1,0:T(8,128)S(1)} %get-tuple-element.6) | copy-start | bytes 1572868
where the time goes:
time: 295 us; the launch traced here: 294 us
  blocking collectives  135 us (46%)
  local copies, waits for them, and re-layouts  51.6 us (17%)
  starting transfers between devices  34.7 us (12%)
  waiting for transfers between devices  33.7 us (11%)
  other arithmetic  21.7 us (7%)
  matrix products  16.9 us (6%)
    psum x1, blocking collectives, per_device(): norm_old = lax.psum(jnp.sum(residual * residual, axis=(1, 2)), ('tx', 'ty'))  72 us
    psum x1, blocking collectives, per_device(): lax.psum(jnp.sum(next_residual * next_residual, axis=(1, 2)), ('tx', 'ty'))  62.5 us
    scatter x1, local copies, waits for them, and re-layouts, per_device(): jnp.zeros((devices * cap, beacons, cells), jnp.float32).at[slot]  23.9 us
    dot_general x1, matrix products, per_device(): jnp.einsum('bsc,bks->bkc', blocks, samples, preferred_element_type=jnp.fl...  16.9 us
    all_to_all x1, waiting for transfers between devices, per_device(): lax.all_to_all(outgoing.reshape(devices, cap, beacons, cells), ('tx', 'ty...  16.6 us
    scatter-add x1, other arithmetic, per_device(): data_tiles = jnp.zeros(own_tiles.shape, jnp.float32).at[wanted].add(arrived)  14.7 us
    ppermute x2, waiting for transfers between devices, padded_2(): after = lax.ppermute(initial, axis, down)  13.9 us
    all_to_all x1, starting transfers between devices, per_device(): lax.all_to_all(request.reshape(devices, cap), ('tx', 'ty'), split_axis=0,...  11.5 us
  transfers between devices with their start and end apart: 7, of which 5 were waited for; matrix products, arithmetic and copies ran while one was open for 3% of the time, Pallas kernels for 0%

commit v1 on v0

--- a/solution.py
+++ b/solution.py
@@ -86,7 +86,9 @@
     arrived = arrived.reshape(devices * cap, beacons, cells)
     data_tiles = jnp.zeros(own_tiles.shape, jnp.float32).at[wanted].add(arrived)
     image = to_field(data_tiles, rows, cols) + smooth_weight * laplace_local(direction)
-    norm_old = lax.psum(jnp.sum(residual * residual, axis=(1, 2)), ("tx", "ty"))
+    norm_old = jnp.sum(
+        lax.all_gather(jnp.sum(residual * residual, axis=(1, 2)), ("tx", "ty")), axis=0
+    )
     curvature = lax.psum(jnp.sum(direction * image, axis=(1, 2)), ("tx", "ty"))
     alpha = norm_old / curvature
     next_residual = residual - alpha[:, None, None] * image

time: 295 us -> 296 us (level)
    psum x1 -> x0, blocking collectives: 72 us -> none  [per_device(): norm_old = lax.psum(jnp.sum(residual * residual, axis=(1, 2)), ('tx', 'ty'))]
    unnamed x0 -> x1, blocking collectives: none -> 72 us
where the time goes in v1:
time: 296 us; the launch traced here: 294 us
  blocking collectives  135 us (46%)
  local copies, waits for them, and re-layouts  51.9 us (18%)
  starting transfers between devices  34.9 us (12%)
  waiting for transfers between devices  33.3 us (11%)
  other arithmetic  21.8 us (7%)
  matrix products  16.9 us (6%)
    unnamed x1, blocking collectives  72 us
    psum x1, blocking collectives, per_device(): lax.psum(jnp.sum(next_residual * next_residual, axis=(1, 2)), ('tx', 'ty'))  62.6 us
    scatter x1, local copies, waits for them, and re-layouts, per_device(): jnp.zeros((devices * cap, beacons, cells), jnp.float32).at[slot]  23.9 us
    dot_general x1, matrix products, per_device(): jnp.einsum('bsc,bks->bkc', blocks, samples, preferred_element_type=jnp.fl...  16.9 us
    all_to_all x1, waiting for transfers between devices, per_device(): lax.all_to_all(outgoing.reshape(devices, cap, beacons, cells), ('tx', 'ty...  16.6 us
    scatter-add x1, other arithmetic, per_device(): data_tiles = jnp.zeros(own_tiles.shape, jnp.float32).at[wanted].add(arrived)  14.7 us
    ppermute x2, waiting for transfers between devices, padded_2(): after = lax.ppermute(initial, axis, down)  13.5 us
    all_to_all x1, starting transfers between devices, per_device(): lax.all_to_all(request.reshape(devices, cap), ('tx', 'ty'), split_axis=0,...  11.5 us
  transfers between devices with their start and end apart: 7, of which 5 were waited for; matrix products, arithmetic and copies ran while one was open for 3% of the time, Pallas kernels for 0%

profile of v1, /device:TPU:1, one launch (start us, length us, event | category | flops | bytes accessed | tf_op | source)
XLA Modules:
  0.0 294.3 jit_solution(5105348849298314274)
XLA Ops:
  3.3 1.6 scatter_custom_fusion
  5.7 11.5 %all-to-all-start = ((s32[128,1,3]{2,1,0:T(1,128)}), s32[128,1,3]{2,1,0:T(1,128)S(1)}, u32[]{:S(2)}, u32[]{:S(2)}) async-start(s32[128,1,3]{2,1,0:T(1,128)} %bitcast.7), calls=%async_computation | async-start | bytes 131072 | tf_op jit(solution)/shard_map/all_to_all | solution.py:59
  18.3 2.5 reshape.85
  20.7 2.1 copy.33
  22.9 2.0 reshape.86
  25.1 1.8 all-to-all-done
  27.7 2.3 gather_fusion
  30.0 1.4 broadcast_select_fusion
  31.4 8.0 %all-to-all-start.1 = ((bf16[128,3,4,256]{3,2,1,0:T(4,128)(2,1)}), bf16[128,3,4,256]{3,2,1,0:T(4,128)(2,1)S(1)}, u32[]{:S(2)}, u32[]{:S(2)}) async-start(bf16[128,3,4,256]{3,2,1,0:T(4,128)(2,1)} %broadcast_select_fusion), calls=%async_computation.1 | async-start | bytes 1572864 | tf_op jit(solution)/shard_map/all_to_all | solution.py:65
  39.5 16.6 %all-to-all-done.1 = bf16[128,3,4,256]{3,2,1,0:T(4,128)(2,1)S(1)} async-done(((bf16[128,3,4,256]{3,2,1,0:T(4,128)(2,1)}), bf16[128,3,4,256]{3,2,1,0:T(4,128)(2,1)S(1)}, u32[]{:S(2)}, u32[]{:S(2)}) %all-to-all-start.1) | async-done | bytes 786464 | tf_op jit(solution)/shard_map/all_to_all | solution.py:65
  57.3 16.9 %fusion = f32[256,4,256]{2,1,0:T(4,128)S(1)} fusion(bf16[256,128,256]{2,1,0:T(8,128)(2,1)} %param.9, bf16[256,4,256]{2,1,0:T(4,128)(2,1)S(1)} %gather_fusion.1, pred[256]{0:T(512)(128)(4,1)S(1)} %get-tuple-element.9), kind=kOutput, calls=%fused_computation.8 | convolution fusion | flops 134610944 | bytes 18350336 | tf_op jit(solution)/shard_map/bsc,bks->bkc/dot_general | solution.py:77
  75.5 23.9 %scatter_fusion = f32[384,4,256]{2,1,0:T(4,128)} fusion(f32[384,4,256]{2,1,0:T(4,128)} %broadcast_in_dim.38, s32[256]{0:T(256)S(1)} %bitcast.49, f32[256,4,256]{2,1,0:T(4,128)S(1)} %fusion), kind=kCustom, calls=%fused_computation.3 | custom fusion | bytes 3146752 | tf_op jit(solution)/shard_map/scatter | solution.py:78
  99.4 4.3 %all-to-all-start.2 = ((f32[128,3,4,256]{3,2,1,0:T(4,128)}), f32[128,3,4,256]{3,2,1,0:T(4,128)S(1)}, u32[]{:S(2)}, u32[]{:S(2)}) async-start(f32[128,3,4,256]{3,2,1,0:T(4,128)} %bitcast.12), calls=%async_computation.2 | async-start | bytes 3145728 | tf_op jit(solution)/shard_map/all_to_all | solution.py:79
  103.7 3.1 %collective-permute-start.1 = (bf16[4,1,256]{2,1,0:T(2,128)(2,1)S(1)}, bf16[4,1,256]{2,1,0:T(2,128)(2,1)S(1)}, u32[]{:S(2)}, u32[]{:S(2)}) collective-permute-start(bf16[4,1,256]{2,1,0:T(2,128)(2,1)S(1)} %get-tuple-element.16), channel_id=1, source_target_pairs={{16,0},{32,16},{48,32},{64,48},{80,64},{96,80},{112,96},{17,1},{33... | collective-permute-start | bytes 6152 | tf_op jit(solution)/shard_map/ppermute | solution.py:18
  106.9 2.4 collective-permute-start
  109.3 13.3 %collective-permute-done.1 = bf16[4,1,256]{2,1,0:T(2,128)(2,1)S(1)} collective-permute-done((bf16[4,1,256]{2,1,0:T(2,128)(2,1)S(1)}, bf16[4,1,256]{2,1,0:T(2,128)(2,1)S(1)}, u32[]{:S(2)}, u32[]{:S(2)}) %collective-permute-start.1) | collective-permute-done | bytes 2080 | tf_op jit(solution)/shard_map/ppermute | solution.py:18
  122.8 1.5 collective-permute-start.3
  124.3 4.0 %collective-permute-start.2 = (bf16[4,130,1]{2,1,0:T(8,128)(2,1)S(1)}, bf16[4,130,1]{2,1,0:T(8,128)(2,1)S(1)}, u32[]{:S(2)}, u32[]{:S(2)}) collective-permute-start(bf16[4,130,1]{2,1,0:T(8,128)(2,1)S(1)} %get-tuple-element.13), channel_id=1, source_target_pairs={{0,1},{1,2},{2,3},{3,4},{4,5},{5,6},{6,7},{7,8},{8,9},{9,10},{10,1... | collective-permute-start | bytes 3128 | tf_op jit(solution)/shard_map/ppermute | solution.py:17
  130.7 14.7 %scatter_fusion.1 = f32[128,4,256]{2,1,0:T(4,128)S(1)} fusion(f32[128,4,256]{2,1,0:T(4,128)S(1)} %broadcast_in_dim.36, s32[384]{0:T(512)S(1)} %reshape.126, f32[384,4,256]{2,1,0:T(4,128)S(1)} %bitcast.39), kind=kCustom, calls=%fused_computation.4 | custom fusion | flops 393216 | bytes 4720128 | tf_op jit(solution)/shard_map/scatter-add | solution.py:87
  145.5 2.6 reshape.90
  148.1 5.9 %copy.31 = f32[4,8,16,16,16]{4,3,2,1,0:T(8,128)} copy(f32[4,8,16,16,16]{4,2,3,1,0:T(8,128)} %bitcast.37) | data formatting | bytes 1048576 | tf_op jit(solution)/shard_map/transpose | solution.py:35
  154.0 3.5 %reshape.91 = f32[4,128,256]{2,1,0:T(8,128)S(1)} reshape(f32[4,8,16,16,16]{4,3,2,1,0:T(8,128)} %copy.31) | data formatting | bytes 1048576 | tf_op jit(solution)/shard_map/reshape | solution.py:36
  158.1 72.0 %all-reduce.1 = (f32[512]{0:T(512)S(1)}, f32[4]{0:T(128)S(1)}) all-reduce(f32[512]{0:T(512)S(1)} %dynamic-update-slice, f32[4]{0:T(128)S(1)} %get-tuple-element.7), channel_id=2, replica_groups=mesh['tx'=8,'ty'=16] {'tx','ty'}, use_global_device_ids=true, to_apply=%add | all-reduce | flops 516 | bytes 4128
  230.6 62.6 %psum.15 = f32[4]{0:T(128)S(1)} all-reduce(f32[4]{0:T(128)S(1)} %get-tuple-element.5), channel_id=1, replica_groups=mesh['tx'=8,'ty'=16] {'tx','ty'}, use_global_device_ids=true, to_apply=%region_11.12 | all-reduce | flops 4 | bytes 32 | tf_op jit(solution)/shard_map/psum | solution.py:95
  (52 shorter events, 12.8 us)
Async XLA Ops:
  5.7 21.2 %all-to-all-start = ((s32[128,1,3]{2,1,0:T(1,128)}), s32[128,1,3]{2,1,0:T(1,128)S(1)}, u32[]{:S(2)}, u32[]{:S(2)}) async-start(s32[128,1,3]{2,1,0:T(1,128)} %bitcast.7), calls=%async_computation | async-start | bytes 131072 | tf_op jit(solution)/shard_map/all_to_all | solution.py:59
  31.4 24.7 %all-to-all-start.1 = ((bf16[128,3,4,256]{3,2,1,0:T(4,128)(2,1)}), bf16[128,3,4,256]{3,2,1,0:T(4,128)(2,1)S(1)}, u32[]{:S(2)}, u32[]{:S(2)}) async-start(bf16[128,3,4,256]{3,2,1,0:T(4,128)(2,1)} %broadcast_select_fusion), calls=%async_computation.1 | async-start | bytes 1572864 | tf_op jit(solution)/shard_map/all_to_all | solution.py:65
  99.4 28.9 %copy-start.2 = (f32[4,128,256]{2,1,0:T(8,128)S(1)}, f32[4,128,256]{2,1,0:T(8,128)}, u32[]{:S(2)}) copy-start(f32[4,128,256]{2,1,0:T(8,128)} %param.7) | copy-start | bytes 1572868
  99.4 31.2 %all-to-all-start.2 = ((f32[128,3,4,256]{3,2,1,0:T(4,128)}), f32[128,3,4,256]{3,2,1,0:T(4,128)S(1)}, u32[]{:S(2)}, u32[]{:S(2)}) async-start(f32[128,3,4,256]{3,2,1,0:T(4,128)} %bitcast.12), calls=%async_computation.2 | async-start | bytes 3145728 | tf_op jit(solution)/shard_map/all_to_all | solution.py:79
  103.7 18.9 %collective-permute-start.1 = (bf16[4,1,256]{2,1,0:T(2,128)(2,1)S(1)}, bf16[4,1,256]{2,1,0:T(2,128)(2,1)S(1)}, u32[]{:S(2)}, u32[]{:S(2)}) collective-permute-start(bf16[4,1,256]{2,1,0:T(2,128)(2,1)S(1)} %get-tuple-element.16), channel_id=1, source_target_pairs={{16,0},{32,16},{48,32},{64,48},{80,64},{96,80},{112,96},{17,1},{33... | collective-permute-start | bytes 6152 | tf_op jit(solution)/shard_map/ppermute | solution.py:18
  106.9 15.7 %collective-permute-start = (bf16[4,1,256]{2,1,0:T(2,128)(2,1)S(1)}, bf16[4,1,256]{2,1,0:T(2,128)(2,1)S(1)}, u32[]{:S(2)}, u32[]{:S(2)}) collective-permute-start(bf16[4,1,256]{2,1,0:T(2,128)(2,1)S(1)} %get-tuple-element.15), channel_id=1, source_target_pairs={{0,16},{16,32},{32,48},{48,64},{64,80},{80,96},{96,112},{1,17},{17... | collective-permute-start | bytes 6152 | tf_op jit(solution)/shard_map/ppermute | solution.py:17
  122.8 6.1 %collective-permute-start.3 = (bf16[4,130,1]{2,1,0:T(8,128)(2,1)S(1)}, bf16[4,130,1]{2,1,0:T(8,128)(2,1)S(1)}, u32[]{:S(2)}, u32[]{:S(2)}) collective-permute-start(bf16[4,130,1]{2,1,0:T(8,128)(2,1)S(1)} %get-tuple-element.14), channel_id=1, source_target_pairs={{1,0},{2,1},{3,2},{4,3},{5,4},{6,5},{7,6},{8,7},{9,8},{10,9},{11,1... | collective-permute-start | bytes 3128 | tf_op jit(solution)/shard_map/ppermute | solution.py:18
  124.3 6.0 %collective-permute-start.2 = (bf16[4,130,1]{2,1,0:T(8,128)(2,1)S(1)}, bf16[4,130,1]{2,1,0:T(8,128)(2,1)S(1)}, u32[]{:S(2)}, u32[]{:S(2)}) collective-permute-start(bf16[4,130,1]{2,1,0:T(8,128)(2,1)S(1)} %get-tuple-element.13), channel_id=1, source_target_pairs={{0,1},{1,2},{2,3},{3,4},{4,5},{5,6},{6,7},{7,8},{8,9},{9,10},{10,1... | collective-permute-start | bytes 3128 | tf_op jit(solution)/shard_map/ppermute | solution.py:17
  154.0 3.6 %copy-start = (f32[4,128,256]{2,1,0:T(8,128)S(1)}, f32[4,128,256]{2,1,0:T(8,128)}, u32[]{:S(2)}) copy-start(f32[4,128,256]{2,1,0:T(8,128)} %param.8) | copy-start | bytes 1572868
  157.5 72.8 %copy-start.3 = (f32[4,128,256]{2,1,0:T(8,128)S(1)}, f32[4,128,256]{2,1,0:T(8,128)}, u32[]{:S(2)}) copy-start(f32[4,128,256]{2,1,0:T(8,128)} %param.7) | copy-start | bytes 1572868
  157.6 135.6 %copy-start.4 = (f32[4,128,256]{2,1,0:T(8,128)S(1)}, f32[4,128,256]{2,1,0:T(8,128)}, u32[]{:S(2)}) copy-start(f32[4,128,256]{2,1,0:T(8,128)} %param.6) | copy-start | bytes 1572868
  230.6 63.8 %copy-start.1 = (f32[4,128,256]{2,1,0:T(8,128)}, f32[4,128,256]{2,1,0:T(8,128)S(1)}, u32[]{:S(2)}) copy-start(f32[4,128,256]{2,1,0:T(8,128)S(1)} %get-tuple-element.6) | copy-start | bytes 1572868
